TPU v7x, 128 devices: a whole 4x4x4 slice. The times are simulated.
128 devices in a mesh: row: 8 (over y, x_hi), col: 16 (over z, x_lo, core).
Axes of the slice: x: 4 (x_hi: 2, x_lo: 2; x = x_hi * 2 + x_lo), y: 4, z: 4, core: 2. Of those that a mesh axis runs over, the one named last changes fastest.
Arguments:
- right_sides: bfloat16 [64, 2097152], P(None, ('row', 'col')), may hold values from -6 to 6
- leaf_factor: bfloat16 [16384, 64, 128], P(('row', 'col')), may hold values from -0.5 to 0.5
- middle_factor: bfloat16 [8, 16384, 64, 128], P(None, ('row', 'col')), may hold values from -0.5 to 0.5
- root_factor: bfloat16 [16384, 64, 128], P(('row', 'col')), may hold values from -0.75 to 0.75
- partners: int32 [8, 128, 128], P(None, ('row', 'col')), may hold values from 0 to 127, each once within a row
- pattern: int32 [8, 128, 128], P(None, ('row', 'col')), may hold values 0 or 1
Outputs:
- applied: bfloat16 [64, 2097152], P(None, ('row', 'col'))
Inputs may be any that keep to these rules, and one draw needn't show every extreme that they name: partners[l, d, :] is a permutation of 0 .. 127 for every level and device.
All inputs are finite; a program needn't handle non-finite values. No bound on the sum of `pattern` on one device may be relied on, other than what follows from the above.
Results may differ from a plain program's by a relative error of at most 0.017.
Values may be sent and summed in bfloat16 or wider, within the bound.
A program may use at most 128 MiB of HBM per device.

v0:
```python
import functools

import jax
import jax.numpy as jnp
from jax import lax
from jax.experimental import pallas as pl
from jax.experimental.pallas import tpu as pltpu
from jax.sharding import PartitionSpec as P

MESH = pl.DeviceIdType.MESH
BF16, F32 = jnp.bfloat16, jnp.float32
CHUNKS = (16, 16, 16, 16)
GROUP = 16
SKEW = 1


def dot_t(a, b):
    return lax.dot_general(a, b, (((1,), (1,)), ((), ())), preferred_element_type=F32)


def task_order(chunks, stages, skew):
    order = []
    for t in range(stages + (chunks - 1) * skew):
        for k in range(chunks):
            if 0 <= t - k * skew < stages:
                order.append((k, t - k * skew))
    return order


def kernel(row_bits, col_bits, chunks, order, *refs):
    refs = list(refs)
    part, pat, x_hbm, leaf_hbm, mid_hbm, root_hbm, out_hbm = refs[:7]
    x, leaf, mid, root, out = refs[7:12]
    x_sem, w_sem, out_sem, send_sem, recv_sem = refs[12:17]
    rest = iter(refs[17:])
    n_chunks = len(chunks)
    starts = [sum(chunks[:k]) for k in range(n_chunks)]
    levels = row_bits + col_bits + 1
    t_stage = row_bits + 1
    first = [next(rest) for _ in chunks]
    state = [[next(rest), next(rest)] for _ in chunks]
    moved = [next(rest) for _ in chunks]
    got = [
        {s: next(rest) for s in range(1, levels + 1) if s != t_stage} for _ in chunks
    ]
    pairs = leaf.shape[0]
    cols = 1 << col_bits
    band = pairs // cols
    r, c = lax.axis_index("row"), lax.axis_index("col")

    def peer(s):
        if s < t_stage:
            return (r ^ (1 << (s - 1)), c)
        return (r, c ^ (1 << (s - t_stage - 1)))

    def rows(k):
        return pl.ds(starts[k], chunks[k])

    def x_copy(k):
        return pltpu.make_async_copy(x_hbm.at[rows(k)], x.at[rows(k)], x_sem.at[k])

    def out_copy(k):
        return pltpu.make_async_copy(
            out.at[rows(k)], out_hbm.at[rows(k)], out_sem.at[k]
        )

    leaf_copy = pltpu.make_async_copy(leaf_hbm, leaf, w_sem.at[levels])
    root_copy = pltpu.make_async_copy(root_hbm, root, w_sem.at[levels + 1])

    def mid_copy(l):
        return pltpu.make_async_copy(mid_hbm.at[l], mid.at[l], w_sem.at[l])

    x_copy(0).start()
    leaf_copy.start()
    mid_copy(0).start()
    for k in range(1, n_chunks):
        x_copy(k).start()
    for l in range(1, levels):
        mid_copy(l).start()
    root_copy.start()

    barrier = pltpu.get_barrier_semaphore()
    for s in range(1, t_stage):
        pl.semaphore_signal(barrier, inc=1, device_id=peer(s), device_id_type=MESH)
    for d in range(1, cols):
        pl.semaphore_signal(barrier, inc=1, device_id=(r, c ^ d), device_id_type=MESH)

    for k in range(n_chunks):
        blank = jnp.zeros((chunks[k], 128), BF16)
        first[k][pairs] = blank
        for s in got[k]:
            got[k][s][pairs] = blank

    def send(k, s, source, at, count):
        return pltpu.make_async_remote_copy(
            src_ref=source.at[pl.ds(at, count)],
            dst_ref=got[k][s].at[pl.ds(at, count)],
            send_sem=send_sem.at[k, s],
            recv_sem=recv_sem.at[k, s],
            device_id=peer(s),
            device_id_type=MESH,
        )

    def move(k, source, d):
        j = c ^ d
        return pltpu.make_async_remote_copy(
            src_ref=source.at[pl.ds(j * band, band)],
            dst_ref=moved[k].at[pl.ds(c * band, band)],
            send_sem=send_sem.at[k, t_stage],
            recv_sem=recv_sem.at[k, t_stage],
            device_id=(r, j),
            device_id_type=MESH,
        )

    def moved_all(k, source):
        count = pairs - band
        return pltpu.make_async_remote_copy(
            src_ref=source.at[pl.ds(0, count)],
            dst_ref=moved[k].at[pl.ds(0, count)],
            send_sem=send_sem.at[k, t_stage],
            recv_sem=recv_sem.at[k, t_stage],
            device_id=(r, c ^ 1),
            device_id_type=MESH,
        )

    def low(k):
        return lax.broadcasted_iota(jnp.int32, (chunks[k], 128), 1) < 64

    def grouped(body, after=None):
        def step(g, carry):
            at = g * GROUP
            body([at + i for i in range(GROUP)])
            if after is not None:
                after(at)
            return carry

        lax.fori_loop(0, pairs // GROUP, step, 0)

    def leaf_task(k):
        n, half = chunks[k], low(k)

        def body(qs):
            ys = []
            for q in qs:
                both = x[rows(k), pl.ds(pl.multiple_of(q * 256, 256), 256)]
                z = jnp.concatenate([both[:, :128], both[:, 128:]], axis=0)
                ys.append(dot_t(z, leaf[q]))
            for q, y in zip(qs, ys):
                first[k][q] = jnp.where(half, y[:n], y[n:]).astype(BF16)

        grouped(body)

    def level_task(k, l, own, other, result, after):
        n, half = chunks[k], low(k)

        def picked(b):
            p, keep = part[l, b], pat[l, b]
            tile = pairs + keep * ((p >> 1) - pairs)
            turn = 1 - (p & 1)
            return pltpu.roll(other[tile], turn * 64, 1)

        def body(qs):
            ys = []
            for q in qs:
                mine = own[q]
                even = jnp.where(half, mine, picked(2 * q))
                odd = jnp.where(half, pltpu.roll(mine, 64, 1), picked(2 * q + 1))
                ys.append(dot_t(jnp.concatenate([even, odd], axis=0), mid[l, q]))
            for q, y in zip(qs, ys):
                result[q] = jnp.where(half, y[:n], y[n:]).astype(BF16)

        grouped(body, after)

    def root_task(k, source):
        n, half = chunks[k], low(k)

        def body(qs):
            ys = []
            for q in qs:
                mine = source[q]
                none = jnp.zeros_like(mine)
                z = jnp.concatenate(
                    [jnp.where(half, mine, none), jnp.where(half, none, mine)], axis=0
                )
                ys.append(jnp.dot(z, root[q], preferred_element_type=F32))
            for q, y in zip(qs, ys):
                y = y.astype(BF16)
                at = pl.multiple_of(q * 256, 256)
                out[rows(k), pl.ds(at, 128)] = y[:n]
                out[rows(k), pl.ds(at + 128, 128)] = y[n:]

        grouped(body)

    ready = set()

    def need(name, copy):
        if name not in ready:
            ready.add(name)
            copy().wait()

    greeted = [False]

    def greet():
        if not greeted[0]:
            greeted[0] = True
            pl.semaphore_wait(barrier, row_bits + cols - 1)

    def sender(k, s, source):
        def after(at):
            send(k, s, source, at, GROUP).start()

        return after

    held = {}
    for k, t in order:
        if t == 0:
            need(("x", k), lambda: x_copy(k))
            need("leaf", lambda: leaf_copy)
            leaf_task(k)
            need(("mid", 0), lambda: mid_copy(0))
            greet()
            level_task(k, 0, first[k], first[k], state[k][0], sender(k, 1, state[k][0]))
            held[k] = state[k][0]
        elif t == t_stage:
            moved_all(k, held[k]).wait_recv()
            held[k] = moved[k]
            send(k, t + 1, moved[k], 0, pairs).start()
        elif t <= levels:
            l = t if t < t_stage else t - 1
            need(("mid", l), lambda: mid_copy(l))
            send(k, t, held[k], 0, pairs).wait_recv()
            result = state[k][l % 2]
            if l >= 2:
                before = l - 1 if l <= t_stage + 1 else l
                if before == t_stage:
                    moved_all(k, result).wait_send()
                else:
                    send(k, before, result, 0, pairs).wait_send()
            if t == t_stage - 1:
                level_task(k, l, held[k], got[k][t], result, None)
                for d in range(1, cols):
                    move(k, result, d).start()
                moved[k][pl.ds(c * band, band)] = result[pl.ds(c * band, band)]
            elif t == levels:
                level_task(k, l, held[k], got[k][t], result, None)
            else:
                level_task(k, l, held[k], got[k][t], result, sender(k, t + 1, result))
            held[k] = result
        else:
            need("root", lambda: root_copy)
            root_task(k, held[k])
            out_copy(k).start()
    for k in range(n_chunks):
        send(k, t_stage + 1, moved[k], 0, pairs).wait_send()
        send(k, levels, state[k][0], 0, pairs).wait_send()
        out_copy(k).wait()


def per_device(right_sides, leaf_factor, middle_factor, root_factor, partners, pattern):
    row_bits = lax.axis_size("row").bit_length() - 1
    col_bits = lax.axis_size("col").bit_length() - 1
    nrhs = right_sides.shape[0]
    blocks, rank, width = leaf_factor.shape
    pairs, levels = blocks // 2, middle_factor.shape[0]
    chunks = CHUNKS
    t_stage = row_bits + 1
    stages = [s for s in range(1, levels + 1) if s != t_stage]
    tiles = [
        pltpu.VMEM((pairs + 1, n, width), BF16) for n in chunks
    ]
    plain = [pltpu.VMEM((pairs, n, width), BF16) for n in chunks]
    scratch = [
        pltpu.VMEM((nrhs, blocks * width), BF16),
        pltpu.VMEM((pairs, 2 * rank, width), BF16),
        pltpu.VMEM((levels, pairs, 2 * rank, width), BF16),
        pltpu.VMEM((pairs, 2 * rank, width), BF16),
        pltpu.VMEM((nrhs, blocks * width), BF16),
        pltpu.SemaphoreType.DMA((len(chunks),)),
        pltpu.SemaphoreType.DMA((levels + 2,)),
        pltpu.SemaphoreType.DMA((len(chunks),)),
        pltpu.SemaphoreType.DMA((len(chunks), levels + 1)),
        pltpu.SemaphoreType.DMA((len(chunks), levels + 1)),
    ]
    scratch += tiles
    for one in plain:
        scratch += [one, one]
    scratch += plain
    for one in tiles:
        scratch += [one] * len(stages)
    order = task_order(len(chunks), levels + 2, SKEW)
    anywhere = pl.BlockSpec(memory_space=pl.ANY)
    scalars = pl.BlockSpec(memory_space=pltpu.SMEM)
    return pl.pallas_call(
        functools.partial(kernel, row_bits, col_bits, chunks, order),
        out_shape=jax.ShapeDtypeStruct(right_sides.shape, BF16),
        in_specs=[scalars, scalars] + [anywhere] * 4,
        out_specs=anywhere,
        scratch_shapes=scratch,
        compiler_params=pltpu.CompilerParams(
            collective_id=0, has_side_effects=True, vmem_limit_bytes=58 << 20
        ),
    )(
        partners.reshape(levels, blocks),
        pattern.reshape(levels, blocks),
        right_sides,
        leaf_factor.reshape(pairs, 2 * rank, width),
        middle_factor.reshape(levels, pairs, 2 * rank, width),
        root_factor.reshape(pairs, 2 * rank, width),
    )


def solution(mesh):
    in_specs = (
        P(None, ("row", "col")),
        P(("row", "col"), None, None),
        P(None, ("row", "col"), None, None),
        P(("row", "col"), None, None),
        P(None, ("row", "col"), None),
        P(None, ("row", "col"), None),
    )
    out_specs = P(None, ("row", "col"))
    return jax.shard_map(
        per_device, mesh=mesh, in_specs=in_specs, out_specs=out_specs, check_vma=False
    )
```

profile of v0, /device:TPU:0, one launch (start us, length us, event | category | flops | bytes accessed | tf_op | source)
XLA Modules:
  0.0 126.0 jit_solution(12992577626364610131)
XLA Ops:
  0.0 122.9 %shard_map.64 = bf16[64,16384]{1,0:T(8,128)(2,1)} custom-call(s32[8,128]{1,0:T(8,128)} %bitcast.8, s32[8,128]{1,0:T(8,128)} %bitcast.9, bf16[64,16384]{1,0:T(8,128)(2,1)} %refs_2_.1, bf16[64,128,128]{2,1,0:T(8,128)(2,1)} %bitcast.6, bf16[8,64,128,128]{3,2,1,0:T(8,128)(2,1)} %bitcast.5, bf16[64,128,128]{2,1,0:T(8,128)(2,1)} %bitcast.7), custom_call_target="tpu_custom_call" | custom-call | tf_op jit(solution)/shard_map/pallas_call | solution.py:293
  122.9 3.0 %copy.8 = bf16[64,16384]{1,0:T(8,128)(2,1)} copy(bf16[64,16384]{1,0:T(8,128)(2,1)} %shard_map.64) | data formatting | bytes 4194304
where the time goes:
time: 126 us
  Pallas kernels  123 us (98%)
  local copies, waits for them, and re-layouts  3.05 us (2%)
    pallas_call x1, Pallas kernels, per_device(): pl.pallas_call(functools.partial(kernel, row_bits, col_bits, chunks, orde...  123 us
    unnamed x1, local copies, waits for them, and re-layouts  3.05 us

commit v1 on v0

--- a/solution.py
+++ b/solution.py
@@ -10,21 +10,29 @@
 MESH = pl.DeviceIdType.MESH
 BF16, F32 = jnp.bfloat16, jnp.float32
 CHUNKS = (16, 16, 16, 16)
-GROUP = 16
-SKEW = 1
-
-
-def dot_t(a, b):
-    return lax.dot_general(a, b, (((1,), (1,)), ((), ())), preferred_element_type=F32)
-
-
-def task_order(chunks, stages, skew):
-    order = []
-    for t in range(stages + (chunks - 1) * skew):
-        for k in range(chunks):
-            if 0 <= t - k * skew < stages:
-                order.append((k, t - k * skew))
-    return order
+GROUP = 32
+ORDER = (
+    (0, 0), (0, 1), (1, 0), (3, 0), (0, 2), (2, 0), (1, 1), (0, 3),
+    (1, 2), (0, 4), (2, 1), (0, 5), (1, 3), (3, 1), (0, 6), (2, 2),
+    (1, 4), (1, 5), (0, 7), (3, 2), (2, 3), (1, 6), (3, 3), (2, 4),
+    (2, 5), (1, 7), (3, 4), (3, 5), (2, 6), (1, 8), (3, 6), (2, 7),
+    (1, 9), (3, 7), (0, 8), (2, 8), (2, 9), (0, 9), (3, 8), (3, 9),
+)
+
+
+def wide(zs, weights, contract):
+    out = []
+    for i in range(0, len(zs), 2):
+        both = jnp.concatenate(weights[i : i + 2], axis=1 - contract)
+        y = lax.dot_general(
+            jnp.concatenate(zs[i : i + 2], axis=0),
+            both,
+            (((1,), (contract,)), ((), ())),
+            preferred_element_type=F32,
+        )
+        rows = zs[i].shape[0]
+        out += [y[:rows, :128], y[rows:, 128:]]
+    return out
 
 
 def kernel(row_bits, col_bits, chunks, order, *refs):
@@ -140,11 +148,11 @@
         n, half = chunks[k], low(k)
 
         def body(qs):
-            ys = []
+            zs = []
             for q in qs:
                 both = x[rows(k), pl.ds(pl.multiple_of(q * 256, 256), 256)]
-                z = jnp.concatenate([both[:, :128], both[:, 128:]], axis=0)
-                ys.append(dot_t(z, leaf[q]))
+                zs.append(jnp.concatenate([both[:, :128], both[:, 128:]], axis=0))
+            ys = wide(zs, [leaf[q] for q in qs], 1)
             for q, y in zip(qs, ys):
                 first[k][q] = jnp.where(half, y[:n], y[n:]).astype(BF16)
 
@@ -160,12 +168,13 @@
             return pltpu.roll(other[tile], turn * 64, 1)
 
         def body(qs):
-            ys = []
+            zs = []
             for q in qs:
                 mine = own[q]
                 even = jnp.where(half, mine, picked(2 * q))
                 odd = jnp.where(half, pltpu.roll(mine, 64, 1), picked(2 * q + 1))
-                ys.append(dot_t(jnp.concatenate([even, odd], axis=0), mid[l, q]))
+                zs.append(jnp.concatenate([even, odd], axis=0))
+            ys = wide(zs, [mid[l, q] for q in qs], 1)
             for q, y in zip(qs, ys):
                 result[q] = jnp.where(half, y[:n], y[n:]).astype(BF16)
 
@@ -175,14 +184,13 @@
         n, half = chunks[k], low(k)
 
         def body(qs):
-            ys = []
+            zs = []
             for q in qs:
                 mine = source[q]
                 none = jnp.zeros_like(mine)
-                z = jnp.concatenate(
-                    [jnp.where(half, mine, none), jnp.where(half, none, mine)], axis=0
-                )
-                ys.append(jnp.dot(z, root[q], preferred_element_type=F32))
+                z = [jnp.where(half, mine, none), jnp.where(half, none, mine)]
+                zs.append(jnp.concatenate(z, axis=0))
+            ys = wide(zs, [root[q] for q in qs], 0)
             for q, y in zip(qs, ys):
                 y = y.astype(BF16)
                 at = pl.multiple_of(q * 256, 256)
@@ -287,7 +295,7 @@
     scratch += plain
     for one in tiles:
         scratch += [one] * len(stages)
-    order = task_order(len(chunks), levels + 2, SKEW)
+    order = ORDER
     anywhere = pl.BlockSpec(memory_space=pl.ANY)
     scalars = pl.BlockSpec(memory_space=pltpu.SMEM)
     return pl.pallas_call(

time: 126 us -> 115 us (0.913)
  Pallas kernels: 123 us -> 112 us
    pallas_call x1, Pallas kernels: 123 us -> 112 us  [per_device(): pl.pallas_call(functools.partial(kernel, row_bits, col_bits, chunks, orde...]
where the time goes in v1:
time: 115 us
  Pallas kernels  112 us (97%)
  local copies, waits for them, and re-layouts  3.05 us (3%)
    pallas_call x1, Pallas kernels, per_device(): pl.pallas_call(functools.partial(kernel, row_bits, col_bits, chunks, orde...  112 us
    unnamed x1, local copies, waits for them, and re-layouts  3.05 us

profile of v1, /device:TPU:0, one launch (start us, length us, event | category | flops | bytes accessed | tf_op | source)
XLA Modules:
  0.0 114.6 jit_solution(15219595838816808255)
XLA Ops:
  0.0 111.5 %shard_map.64 = bf16[64,16384]{1,0:T(8,128)(2,1)} custom-call(s32[8,128]{1,0:T(8,128)} %bitcast.8, s32[8,128]{1,0:T(8,128)} %bitcast.9, bf16[64,16384]{1,0:T(8,128)(2,1)} %refs_2_.1, bf16[64,128,128]{2,1,0:T(8,128)(2,1)} %bitcast.6, bf16[8,64,128,128]{3,2,1,0:T(8,128)(2,1)} %bitcast.5, bf16[64,128,128]{2,1,0:T(8,128)(2,1)} %bitcast.7), custom_call_target="tpu_custom_call" | custom-call | tf_op jit(solution)/shard_map/pallas_call | solution.py:301
  111.5 3.0 %copy.8 = bf16[64,16384]{1,0:T(8,128)(2,1)} copy(bf16[64,16384]{1,0:T(8,128)(2,1)} %shard_map.64) | data formatting | bytes 4194304

commit v2 on v1

--- a/solution.py
+++ b/solution.py
@@ -9,14 +9,17 @@
 
 MESH = pl.DeviceIdType.MESH
 BF16, F32 = jnp.bfloat16, jnp.float32
-CHUNKS = (16, 16, 16, 16)
+CHUNKS = (8, 8, 16, 16, 8, 8)
 GROUP = 32
 ORDER = (
-    (0, 0), (0, 1), (1, 0), (3, 0), (0, 2), (2, 0), (1, 1), (0, 3),
-    (1, 2), (0, 4), (2, 1), (0, 5), (1, 3), (3, 1), (0, 6), (2, 2),
-    (1, 4), (1, 5), (0, 7), (3, 2), (2, 3), (1, 6), (3, 3), (2, 4),
-    (2, 5), (1, 7), (3, 4), (3, 5), (2, 6), (1, 8), (3, 6), (2, 7),
-    (1, 9), (3, 7), (0, 8), (2, 8), (2, 9), (0, 9), (3, 8), (3, 9),
+    (1, 0), (0, 0), (2, 0), (4, 0), (1, 1), (0, 1), (1, 2), (5, 0),
+    (2, 1), (0, 2), (1, 3), (3, 0), (2, 2), (5, 1), (1, 4), (4, 1),
+    (0, 3), (1, 5), (2, 3), (0, 4), (0, 5), (5, 2), (1, 6), (3, 1),
+    (2, 4), (0, 6), (5, 3), (2, 5), (4, 2), (1, 7), (0, 7), (3, 2),
+    (4, 3), (2, 6), (1, 8), (3, 3), (4, 4), (4, 5), (2, 7), (5, 4),
+    (5, 5), (0, 8), (1, 9), (3, 4), (4, 6), (3, 5), (2, 8), (5, 6),
+    (2, 9), (0, 9), (4, 7), (3, 6), (5, 7), (3, 7), (4, 8), (5, 8),
+    (4, 9), (5, 9), (3, 8), (3, 9),
 )
 
 
@@ -37,10 +40,10 @@
 
 def kernel(row_bits, col_bits, chunks, order, *refs):
     refs = list(refs)
-    part, pat, x_hbm, leaf_hbm, mid_hbm, root_hbm, out_hbm = refs[:7]
-    x, leaf, mid, root, out = refs[7:12]
-    x_sem, w_sem, out_sem, send_sem, recv_sem = refs[12:17]
-    rest = iter(refs[17:])
+    part, pat, x_hbm, leaf_hbm, mid_hbm, root_hbm, out = refs[:7]
+    x, leaf, mid, root = refs[7:11]
+    x_sem, w_sem, send_sem, recv_sem = refs[11:15]
+    rest = iter(refs[15:])
     n_chunks = len(chunks)
     starts = [sum(chunks[:k]) for k in range(n_chunks)]
     levels = row_bits + col_bits + 1
@@ -64,13 +67,14 @@
     def rows(k):
         return pl.ds(starts[k], chunks[k])
 
-    def x_copy(k):
-        return pltpu.make_async_copy(x_hbm.at[rows(k)], x.at[rows(k)], x_sem.at[k])
-
-    def out_copy(k):
-        return pltpu.make_async_copy(
-            out.at[rows(k)], out_hbm.at[rows(k)], out_sem.at[k]
-        )
+    n_bands = sum(chunks) // 16
+
+    def bands(k):
+        return range(starts[k] // 16, (starts[k] + chunks[k] - 1) // 16 + 1)
+
+    def x_copy(i):
+        at = pl.ds(i * 16, 16)
+        return pltpu.make_async_copy(x_hbm.at[at], x.at[at], x_sem.at[i])
 
     leaf_copy = pltpu.make_async_copy(leaf_hbm, leaf, w_sem.at[levels])
     root_copy = pltpu.make_async_copy(root_hbm, root, w_sem.at[levels + 1])
@@ -78,11 +82,14 @@
     def mid_copy(l):
         return pltpu.make_async_copy(mid_hbm.at[l], mid.at[l], w_sem.at[l])
 
-    x_copy(0).start()
+    x_first = order[0][0]
+    for i in bands(x_first):
+        x_copy(i).start()
     leaf_copy.start()
     mid_copy(0).start()
-    for k in range(1, n_chunks):
-        x_copy(k).start()
+    for i in range(n_bands):
+        if i not in bands(x_first):
+            x_copy(i).start()
     for l in range(1, levels):
         mid_copy(l).start()
     root_copy.start()
@@ -222,7 +229,8 @@
     held = {}
     for k, t in order:
         if t == 0:
-            need(("x", k), lambda: x_copy(k))
+            for i in bands(k):
+                need(("x", i), lambda: x_copy(i))
             need("leaf", lambda: leaf_copy)
             leaf_task(k)
             need(("mid", 0), lambda: mid_copy(0))
@@ -257,11 +265,9 @@
         else:
             need("root", lambda: root_copy)
             root_task(k, held[k])
-            out_copy(k).start()
     for k in range(n_chunks):
         send(k, t_stage + 1, moved[k], 0, pairs).wait_send()
         send(k, levels, state[k][0], 0, pairs).wait_send()
-        out_copy(k).wait()
 
 
 def per_device(right_sides, leaf_factor, middle_factor, root_factor, partners, pattern):
@@ -282,10 +288,8 @@
         pltpu.VMEM((pairs, 2 * rank, width), BF16),
         pltpu.VMEM((levels, pairs, 2 * rank, width), BF16),
         pltpu.VMEM((pairs, 2 * rank, width), BF16),
-        pltpu.VMEM((nrhs, blocks * width), BF16),
-        pltpu.SemaphoreType.DMA((len(chunks),)),
+        pltpu.SemaphoreType.DMA((nrhs // 16,)),
         pltpu.SemaphoreType.DMA((levels + 2,)),
-        pltpu.SemaphoreType.DMA((len(chunks),)),
         pltpu.SemaphoreType.DMA((len(chunks), levels + 1)),
         pltpu.SemaphoreType.DMA((len(chunks), levels + 1)),
     ]
@@ -300,12 +304,12 @@
     scalars = pl.BlockSpec(memory_space=pltpu.SMEM)
     return pl.pallas_call(
         functools.partial(kernel, row_bits, col_bits, chunks, order),
-        out_shape=jax.ShapeDtypeStruct(right_sides.shape, BF16),
+        out_shape=pltpu.VMEM(right_sides.shape, BF16),
         in_specs=[scalars, scalars] + [anywhere] * 4,
-        out_specs=anywhere,
+        out_specs=pl.BlockSpec(memory_space=pltpu.VMEM),
         scratch_shapes=scratch,
         compiler_params=pltpu.CompilerParams(
-            collective_id=0, has_side_effects=True, vmem_limit_bytes=58 << 20
+            collective_id=0, has_side_effects=True, vmem_limit_bytes=60 << 20
         ),
     )(
         partners.reshape(levels, blocks),

time: 115 us -> 109 us (0.948)
  Pallas kernels: 112 us -> 107 us
  local copies, waits for them, and re-layouts: 3.05 us -> 1.32 us
    pallas_call x1, Pallas kernels: 112 us -> 107 us  [per_device(): pl.pallas_call(functools.partial(kernel, row_bits, col_bits, chunks, orde...]
    unnamed x1, local copies, waits for them, and re-layouts: 3.05 us -> 1.32 us
where the time goes in v2:
time: 109 us; the launch traced here: 108 us
  Pallas kernels  107 us (98%)
  local copies, waits for them, and re-layouts  1.32 us (1%)
    pallas_call x1, Pallas kernels, per_device(): pl.pallas_call(functools.partial(kernel, row_bits, col_bits, chunks, orde...  107 us

profile of v2, /device:TPU:0, one launch (start us, length us, event | category | flops | bytes accessed | tf_op | source)
XLA Modules:
  0.0 108.5 jit_solution(14947256742496519345)
XLA Ops:
  0.0 107.1 %shard_map.64 = bf16[64,16384]{1,0:T(8,128)(2,1)S(1)} custom-call(s32[8,128]{1,0:T(8,128)} %bitcast.8, s32[8,128]{1,0:T(8,128)} %bitcast.9, bf16[64,16384]{1,0:T(8,128)(2,1)} %refs_2_.1, bf16[64,128,128]{2,1,0:T(8,128)(2,1)} %bitcast.6, bf16[8,64,128,128]{3,2,1,0:T(8,128)(2,1)} %bitcast.5, bf16[64,128,128]{2,1,0:T(8,128)(2,1)} %bitcast.7), custom_call_target="tpu_custom_call" | custom-call | tf_op jit(solution)/shard_map/pallas_call | solution.py:305
  107.1 1.3 %copy.8 = bf16[64,16384]{1,0:T(8,128)(2,1)} copy(bf16[64,16384]{1,0:T(8,128)(2,1)S(1)} %shard_map.64) | data formatting | bytes 4194304

commit v3 on v2

--- a/solution.py
+++ b/solution.py
@@ -12,14 +12,14 @@
 CHUNKS = (8, 8, 16, 16, 8, 8)
 GROUP = 32
 ORDER = (
-    (1, 0), (0, 0), (2, 0), (4, 0), (1, 1), (0, 1), (1, 2), (5, 0),
-    (2, 1), (0, 2), (1, 3), (3, 0), (2, 2), (5, 1), (1, 4), (4, 1),
-    (0, 3), (1, 5), (2, 3), (0, 4), (0, 5), (5, 2), (1, 6), (3, 1),
-    (2, 4), (0, 6), (5, 3), (2, 5), (4, 2), (1, 7), (0, 7), (3, 2),
-    (4, 3), (2, 6), (1, 8), (3, 3), (4, 4), (4, 5), (2, 7), (5, 4),
-    (5, 5), (0, 8), (1, 9), (3, 4), (4, 6), (3, 5), (2, 8), (5, 6),
-    (2, 9), (0, 9), (4, 7), (3, 6), (5, 7), (3, 7), (4, 8), (5, 8),
-    (4, 9), (5, 9), (3, 8), (3, 9),
+    (0, 0), (1, 0), (3, 0), (4, 0), (0, 1), (1, 1), (0, 2), (5, 0),
+    (3, 1), (0, 3), (1, 2), (2, 0), (3, 2), (0, 4), (4, 1), (0, 5),
+    (1, 3), (5, 1), (0, 6), (3, 3), (1, 4), (4, 2), (0, 7), (1, 5),
+    (5, 2), (4, 3), (3, 4), (2, 1), (1, 6), (3, 5), (5, 3), (4, 4),
+    (1, 7), (2, 2), (3, 6), (4, 5), (0, 8), (5, 4), (2, 3), (1, 8),
+    (5, 5), (4, 6), (0, 9), (3, 7), (2, 4), (1, 9), (2, 5), (4, 7),
+    (5, 6), (2, 6), (3, 8), (4, 8), (5, 7), (2, 7), (5, 8), (5, 9),
+    (4, 9), (3, 9), (2, 8), (2, 9),
 )
 
 

time: 109 us -> 106 us (0.972)
  Pallas kernels: 107 us -> 105 us
    pallas_call x1, Pallas kernels: 107 us -> 105 us  [per_device(): pl.pallas_call(functools.partial(kernel, row_bits, col_bits, chunks, orde...]
where the time goes in v3:
time: 106 us
  Pallas kernels  105 us (99%)
  local copies, waits for them, and re-layouts  1.32 us (1%)
    pallas_call x1, Pallas kernels, per_device(): pl.pallas_call(functools.partial(kernel, row_bits, col_bits, chunks, orde...  105 us

profile of v3, /device:TPU:0, one launch (start us, length us, event | category | flops | bytes accessed | tf_op | source)
XLA Modules:
  0.0 106.3 jit_solution(4046385366995303856)
XLA Ops:
  0.0 105.0 %shard_map.64 = bf16[64,16384]{1,0:T(8,128)(2,1)S(1)} custom-call(s32[8,128]{1,0:T(8,128)} %bitcast.8, s32[8,128]{1,0:T(8,128)} %bitcast.9, bf16[64,16384]{1,0:T(8,128)(2,1)} %refs_2_.1, bf16[64,128,128]{2,1,0:T(8,128)(2,1)} %bitcast.6, bf16[8,64,128,128]{3,2,1,0:T(8,128)(2,1)} %bitcast.5, bf16[64,128,128]{2,1,0:T(8,128)(2,1)} %bitcast.7), custom_call_target="tpu_custom_call" | custom-call | tf_op jit(solution)/shard_map/pallas_call | solution.py:305
  105.0 1.3 %copy.8 = bf16[64,16384]{1,0:T(8,128)(2,1)} copy(bf16[64,16384]{1,0:T(8,128)(2,1)S(1)} %shard_map.64) | data formatting | bytes 4194304

commit v4 on v3

--- a/solution.py
+++ b/solution.py
@@ -87,18 +87,18 @@
         x_copy(i).start()
     leaf_copy.start()
     mid_copy(0).start()
+    barrier = pltpu.get_barrier_semaphore()
+    for s in range(1, t_stage):
+        pl.semaphore_signal(barrier, inc=1, device_id=peer(s), device_id_type=MESH)
+    for d in range(1, cols):
+        pl.semaphore_signal(barrier, inc=1, device_id=(r, c ^ d), device_id_type=MESH)
+
     for i in range(n_bands):
         if i not in bands(x_first):
             x_copy(i).start()
     for l in range(1, levels):
         mid_copy(l).start()
     root_copy.start()
-
-    barrier = pltpu.get_barrier_semaphore()
-    for s in range(1, t_stage):
-        pl.semaphore_signal(barrier, inc=1, device_id=peer(s), device_id_type=MESH)
-    for d in range(1, cols):
-        pl.semaphore_signal(barrier, inc=1, device_id=(r, c ^ d), device_id_type=MESH)
 
     for k in range(n_chunks):
         blank = jnp.zeros((chunks[k], 128), BF16)

time: 106 us -> 104 us (0.981)
  Pallas kernels: 105 us -> 103 us
    pallas_call x1, Pallas kernels: 105 us -> 103 us  [per_device(): pl.pallas_call(functools.partial(kernel, row_bits, col_bits, chunks, orde...]
where the time goes in v4:
time: 104 us
  Pallas kernels  103 us (99%)
  local copies, waits for them, and re-layouts  1.32 us (1%)
    pallas_call x1, Pallas kernels, per_device(): pl.pallas_call(functools.partial(kernel, row_bits, col_bits, chunks, orde...  103 us

profile of v4, /device:TPU:0, one launch (start us, length us, event | category | flops | bytes accessed | tf_op | source)
XLA Modules:
  0.0 103.9 jit_solution(16240058278240513839)
XLA Ops:
  0.0 102.6 %shard_map.64 = bf16[64,16384]{1,0:T(8,128)(2,1)S(1)} custom-call(s32[8,128]{1,0:T(8,128)} %bitcast.8, s32[8,128]{1,0:T(8,128)} %bitcast.9, bf16[64,16384]{1,0:T(8,128)(2,1)} %refs_2_.1, bf16[64,128,128]{2,1,0:T(8,128)(2,1)} %bitcast.6, bf16[8,64,128,128]{3,2,1,0:T(8,128)(2,1)} %bitcast.5, bf16[64,128,128]{2,1,0:T(8,128)(2,1)} %bitcast.7), custom_call_target="tpu_custom_call" | custom-call | tf_op jit(solution)/shard_map/pallas_call | solution.py:305
  102.6 1.3 %copy.8 = bf16[64,16384]{1,0:T(8,128)(2,1)} copy(bf16[64,16384]{1,0:T(8,128)(2,1)S(1)} %shard_map.64) | data formatting | bytes 4194304
